TPU v7x, 32 devices: a whole 2x2x4 slice. The times are simulated.
32 devices in a mesh: dp: 8 (over y, x, core), seq: 4 (over z).
Axes of the slice: x: 2, y: 2, z: 4, core: 2. Of those that a mesh axis runs over, the one named last changes fastest.
Arguments:
- inputs: bfloat16 [16, 2048, 1024], P('dp', 'seq'), may hold values from -8 to 8
- w_qkv: bfloat16 [1024, 3072], replicated, may hold values from -0.1875 to 0.1875
- w_out: bfloat16 [1024, 1024], replicated, may hold values from -0.75 to 0.75
- w_gate_up: bfloat16 [1024, 5504], replicated, may hold values from -0.1875 to 0.1875
- w_down: bfloat16 [1024, 2752], replicated, may hold values from -0.15625 to 0.15625
- gain_attn: float32 [1024], replicated, may hold values from 0.5 to 1.5
- gain_mlp: float32 [1024], replicated, may hold values from 0.5 to 1.5
- doc_start: int32 [16, 2048], P('dp', 'seq'), may hold values from 0 to 2047, as said below
- cotangent: bfloat16 [16, 2048, 1024], P('dp', 'seq'), may hold values from -8 to 8
Outputs:
- outputs: bfloat16 [16, 2048, 1024], P('dp', 'seq')
- grad_inputs: float32 [16, 2048, 1024], P('dp', 'seq')
- grad_qkv: float32 [1024, 3072], P('seq')
- grad_out: float32 [1024, 1024], P('seq')
- grad_gate_up: float32 [1024, 5504], P('seq')
- grad_down: float32 [1024, 2752], P('seq')
- grad_gain_attn: float32 [1024], P('seq')
- grad_gain_mlp: float32 [1024], P('seq')
Inputs may be any that keep to these rules, and one draw needn't show every extreme that they name: doc_start[r, 0] = 0, and doc_start[r, i] is either i or doc_start[r, i - 1]. Of the 2 rows of each index of dp, one holds a single document from some position below 512 to the row's end.
All inputs are finite; a program needn't handle non-finite values.
Results may differ from a plain program's by a relative error of at most 0.019.
Values may be sent and summed in bfloat16 or wider, within the bound.
No kernel may reach another device: no remote copies, remote signals or barrier semaphores. Data moves between devices by JAX's collectives and lax.ppermute only.
A program may use at most 320 MiB of HBM per device.

v0:
```python
import jax
import jax.numpy as jnp
from jax import lax
from jax.sharding import PartitionSpec as P

HEADS = 16
HEAD_DIM = 64
FF = 2752
WINDOW = 64


epsilon = 1e-05
masked_value = -1e30


def shifted(value, axis, steps):
    count = lax.axis_size(axis)
    leading, last = (max(0, -steps), min(count, count - steps))
    return lax.ppermute(value, axis, [(source, source + steps) for source in range(leading, last)])


def contract(left, right, left_dim, right_dim):
    return lax.dot_general(
        left, right, (((left_dim,), (right_dim,)), ((), ())), preferred_element_type=jnp.float32
    )


def masked_scores(queries, keys, allowed, scale):
    scores = (
        jnp.einsum("rqhe,rkhe->rhqk", queries, keys, preferred_element_type=jnp.float32) * scale
    )
    return jnp.where(allowed[:, None], scores, masked_value)


def norm_back(grad_norm, values, inv_rms, gain):
    scaled = grad_norm * gain
    gain_grad = jnp.sum(grad_norm * values * inv_rms, axis=0)
    input_grad = inv_rms * scaled - values * inv_rms**3 * jnp.mean(
        scaled * values, axis=-1, keepdims=True
    )
    return (input_grad, gain_grad)


def per_device(inputs, w_qkv, w_out, w_gate_up, w_down, gain_attn, gain_mlp, doc_start, cotangent):
    rows, group, width = inputs.shape
    tokens = rows * group
    scale = HEAD_DIM ** (-0.5)
    first_pos = lax.axis_index("seq") * group
    query_pos = first_pos + jnp.arange(group, dtype=jnp.int32)
    key_pos = first_pos - WINDOW + jnp.arange(WINDOW + group, dtype=jnp.int32)
    allowed = (key_pos[None, None, :] >= doc_start[:, :, None]) & (
        key_pos[None, None, :] <= query_pos[None, :, None]
    )
    allowed = allowed & (query_pos[None, :, None] - key_pos[None, None, :] <= WINDOW)
    flat = inputs.reshape(tokens, width).astype(jnp.float32)
    inv_one = lax.rsqrt(jnp.mean(flat * flat, axis=-1, keepdims=True) + epsilon)
    normed_one = (flat * inv_one * gain_attn).astype(jnp.bfloat16)
    qkv_all = jnp.dot(normed_one, w_qkv, preferred_element_type=jnp.float32).astype(jnp.bfloat16)
    queries = qkv_all[:, :width].reshape(rows, group, HEADS, HEAD_DIM)
    own_kv = qkv_all[:, width:].reshape(rows, group, 2 * width)
    rim_kv = shifted(own_kv[:, group - WINDOW :], "seq", 1)
    both_kv = jnp.concatenate([rim_kv, own_kv], axis=1)
    keys = both_kv[..., :width].reshape(rows, WINDOW + group, HEADS, HEAD_DIM)
    values = both_kv[..., width:].reshape(rows, WINDOW + group, HEADS, HEAD_DIM)
    scores = masked_scores(queries, keys, allowed, scale)
    row_top = jnp.max(scores, axis=-1, keepdims=True)
    log_total = row_top + jnp.log(jnp.sum(jnp.exp(scores - row_top), axis=-1, keepdims=True))
    probs = jnp.exp(scores - log_total).astype(jnp.bfloat16)
    attended = jnp.einsum("rhqk,rkhe->rqhe", probs, values, preferred_element_type=jnp.float32)
    attended = attended.reshape(tokens, width).astype(jnp.bfloat16)
    resid = flat + jnp.dot(attended, w_out, preferred_element_type=jnp.float32)
    inv_two = lax.rsqrt(jnp.mean(resid * resid, axis=-1, keepdims=True) + epsilon)
    normed_two = (resid * inv_two * gain_mlp).astype(jnp.bfloat16)
    gate_up = jnp.dot(normed_two, w_gate_up, preferred_element_type=jnp.float32)
    gate_act = gate_up[:, :FF]
    up_act = gate_up[:, FF:]
    sigma = jax.nn.sigmoid(gate_act)
    silu_gate = gate_act * sigma
    hidden = (silu_gate * up_act).astype(jnp.bfloat16)
    outputs = (
        (resid + contract(hidden, w_down, 1, 1)).astype(jnp.bfloat16).reshape(rows, group, width)
    )
    grad_rows = cotangent.reshape(tokens, width)
    grad_down = contract(grad_rows, hidden, 0, 0)
    grad_hidden = jnp.dot(grad_rows, w_down, preferred_element_type=jnp.float32)
    grad_gate = grad_hidden * up_act * sigma * (1.0 + gate_act * (1.0 - sigma))
    grad_up = grad_hidden * silu_gate
    grad_gu = jnp.concatenate([grad_gate, grad_up], axis=1).astype(jnp.bfloat16)
    grad_gate_up = contract(normed_two, grad_gu, 0, 0)
    grad_resid_in, grad_gain_mlp = norm_back(
        contract(grad_gu, w_gate_up, 1, 1), resid, inv_two, gain_mlp
    )
    grad_resid = grad_rows.astype(jnp.float32) + grad_resid_in
    grad_branch = grad_resid.astype(jnp.bfloat16)
    grad_out = contract(attended, grad_branch, 0, 0)
    grad_attended = (
        contract(grad_branch, w_out, 1, 1)
        .astype(jnp.bfloat16)
        .reshape(rows, group, HEADS, HEAD_DIM)
    )
    prob_full = jnp.exp(masked_scores(queries, keys, allowed, scale) - log_total)
    grad_probs = jnp.einsum(
        "rqhe,rkhe->rhqk", grad_attended, values, preferred_element_type=jnp.float32
    )
    weighted = jnp.sum(prob_full * grad_probs, axis=-1, keepdims=True)
    grad_scores = (prob_full * (grad_probs - weighted)).astype(jnp.bfloat16)
    grad_queries = (
        jnp.einsum("rhqk,rkhe->rqhe", grad_scores, keys, preferred_element_type=jnp.float32) * scale
    )
    grad_keys = (
        jnp.einsum("rhqk,rqhe->rkhe", grad_scores, queries, preferred_element_type=jnp.float32)
        * scale
    )
    grad_values = jnp.einsum(
        "rhqk,rqhe->rkhe", probs, grad_attended, preferred_element_type=jnp.float32
    )
    grad_kv = jnp.concatenate(
        [
            grad_keys.reshape(rows, WINDOW + group, width),
            grad_values.reshape(rows, WINDOW + group, width),
        ],
        axis=-1,
    )
    returned = shifted(grad_kv[:, :WINDOW].astype(jnp.bfloat16), "seq", -1).astype(jnp.float32)
    own_grad = grad_kv[:, WINDOW:]
    own_grad = jnp.concatenate(
        [own_grad[:, : group - WINDOW], own_grad[:, group - WINDOW :] + returned], axis=1
    )
    grad_qkv_rows = jnp.concatenate(
        [grad_queries.reshape(tokens, width), own_grad.reshape(tokens, 2 * width)], axis=1
    ).astype(jnp.bfloat16)
    grad_qkv = contract(normed_one, grad_qkv_rows, 0, 0)
    grad_flat, grad_gain_attn = norm_back(
        contract(grad_qkv_rows, w_qkv, 1, 1), flat, inv_one, gain_attn
    )
    grad_inputs = (grad_resid + grad_flat).reshape(rows, group, width)
    shares = (
        lax.psum_scatter(
            grad_qkv.astype(jnp.bfloat16), "seq", scatter_dimension=0, tiled=True
        ).astype(jnp.float32),
        lax.psum_scatter(
            grad_out.astype(jnp.bfloat16), "seq", scatter_dimension=0, tiled=True
        ).astype(jnp.float32),
        lax.psum_scatter(
            grad_gate_up.astype(jnp.bfloat16), "seq", scatter_dimension=0, tiled=True
        ).astype(jnp.float32),
        lax.psum_scatter(
            grad_down.astype(jnp.bfloat16), "seq", scatter_dimension=0, tiled=True
        ).astype(jnp.float32),
        lax.psum_scatter(
            grad_gain_attn.astype(jnp.bfloat16), "seq", scatter_dimension=0, tiled=True
        ).astype(jnp.float32),
        lax.psum_scatter(
            grad_gain_mlp.astype(jnp.bfloat16), "seq", scatter_dimension=0, tiled=True
        ).astype(jnp.float32),
    )
    totals = (
        lax.psum(shares[0].astype(jnp.bfloat16), "dp").astype(jnp.float32),
        lax.psum(shares[1].astype(jnp.bfloat16), "dp").astype(jnp.float32),
        lax.psum(shares[2].astype(jnp.bfloat16), "dp").astype(jnp.float32),
        lax.psum(shares[3].astype(jnp.bfloat16), "dp").astype(jnp.float32),
        lax.psum(shares[4].astype(jnp.bfloat16), "dp").astype(jnp.float32),
        lax.psum(shares[5].astype(jnp.bfloat16), "dp").astype(jnp.float32),
    )
    return (outputs, grad_inputs, totals[0], totals[1], totals[2], totals[3], totals[4], totals[5])


def solution(mesh):
    in_specs = (
        P("dp", "seq", None),
        P(),
        P(),
        P(),
        P(),
        P(),
        P(),
        P("dp", "seq"),
        P("dp", "seq", None),
    )
    out_specs = (
        P("dp", "seq", None),
        P("dp", "seq", None),
        P("seq", None),
        P("seq", None),
        P("seq", None),
        P("seq", None),
        P("seq"),
        P("seq"),
    )
    return jax.shard_map(
        per_device, mesh=mesh, in_specs=in_specs, out_specs=out_specs, check_vma=False
    )
```

profile of v0, /device:TPU:0, one launch (start us, length us, event | category | flops | bytes accessed | tf_op | source)
XLA Modules:
  0.0 801.4 jit_solution(15966688290650436273)
XLA Ops:
  7.2 2.2 fusion.6
  9.5 0.6 copy-done.25
  10.1 2.2 fusion.8
  12.3 1.3 copy-done.18
  13.6 7.1 convolution_convert_fusion.3
  21.1 2.2 copy-done.11
  23.4 2.0 copy-done.6
  25.4 0.8 slice.46
  26.2 5.2 collective-permute-start
  31.4 3.1 slice.49
  34.5 6.3 reshape.202
  40.8 5.5 copy.43
  46.7 0.6 and_and_fusion
  47.3 4.2 pad_maximum_fusion.8
  51.6 4.3 copy.42
  55.9 4.3 copy.40
  60.2 17.4 %fusion = (f32[2,16,512]{2,1,0:T(8,128)S(1)}, f32[2,16,512,576]{2,3,1,0:T(8,128)}) fusion(pred[2,512,576]{1,2,0:T(8,128)(4,1)S(1)} %and_and_fusion, bf16[2,512,16,64]{1,3,2,0:T(8,128)(2,1)} %copy.43, bf16[2,576,16,64]{1,3,2,0:T(8,128)(2,1)} %bitcast.80), kind=kOutput, calls=%fused_computation.5 | convolution fusion | flops 1236254720 | bytes 42860544 | tf_op jit(solution)/shard_map/rqhe,rkhe->rhqk/dot_general | solution.py:30
  77.6 16.6 %exponential_reduce_fusion = f32[2,16,512]{2,1,0:T(8,128)S(1)} fusion(f32[2,16,512,576]{2,3,1,0:T(8,128)} %get-tuple-element.30, f32[2,16,512]{2,1,0:T(8,128)S(1)} %get-tuple-element.29, pred[2,512,576]{1,2,0:T(8,128)(4,1)S(1)} %and_and_fusion), kind=kLoop, calls=%fused_computation.3 | loop fusion | flops 37732352 | bytes 38469632 | tf_op jit(solution)/shard_map/reduce_sum | solution.py:67
  94.2 18.2 %convert_bitcast_fusion = bf16[2,512,16,64]{1,3,2,0:T(8,128)(2,1)} fusion(bf16[2,576,16,64]{1,3,2,0:T(8,128)(2,1)} %bitcast.82, f32[2,16,512,576]{2,3,1,0:T(8,128)} %get-tuple-element.30, f32[2,16,512]{2,1,0:T(8,128)S(1)} %log_add_fusion, pred[2,512,576]{1,2,0:T(8,128)(4,1)S(1)} %and_and_fusion), kind=kOutput, calls=%fused_computation.54 | convolution fusion | flops 1246756864 | bytes 42860544 | tf_op jit(solution)/shard_map/rhqk,rkhe->rqhe/dot_general | solution.py:69
  112.4 3.9 copy.44
  117.0 2.8 multiply_reduce_fusion.3
  119.8 20.6 %fusion.34 = f32[1024,5504]{1,0:T(8,128)} fusion(bf16[1024,5504]{1,0:T(8,128)(2,1)} %param.12, f32[1024,1024]{1,0:T(8,128)S(1)} %get-tuple-element.32, f32[1024]{0:T(1024)S(1)} %copy-done.31, f32[1024]{0:T(1024)S(1)} %get-tuple-element.28), kind=kOutput, calls=%fused_computation.83 | convolution fusion | flops 11545870336 | bytes 38019072 | tf_op jit(solution)/shard_map/dot_general | solution.py:74
  140.4 19.4 %multiply_convert_fusion.2 = (bf16[1024,2752]{1,0:T(8,128)(2,1)}, bf16[1024,2752]{1,0:T(8,128)(2,1)}, bf16[1024,2752]{1,0:T(8,128)(2,1)}) fusion(f32[1024,5504]{1,0:T(8,128)} %fusion.34, bf16[1024,1024]{1,0:T(8,128)(2,1)} %bitcast.93, bf16[1024,2752]{0,1:T(8,128)(2,1)} %param.13), kind=kOutput, calls=%fused_computation.8 | convolution fusion | flops 5813633024 | bytes 47185920 | tf_op jit(solution)/shard_map/dot_general | solution.py:85
  159.8 22.3 %multiply_reduce_fusion.1 = (bf16[1024]{0:T(1024)(128)(2,1)}, f32[1024]{0:T(1024)S(1)}, f32[1024,1024]{1,0:T(8,128)}) fusion(f32[1024,1024]{1,0:T(8,128)} %copy-done.14, f32[1024]{0:T(1024)S(1)} %get-tuple-element.28, f32[1024]{0:T(1024)S(1)} %copy-done.31, bf16[1024,5504]{1,0:T(8,128)(2,1)} %param.12, bf16[1024,2752]{1,0:T(8,128)(2,1)} %get-tuple-element.21, ...), kind=kOutput, calls=%fused_computation.42 | convolution fusion | flops 11571558400 | bytes 30947328 | tf_op jit(solution)/shard_map/dot_general | solution.py:23
  182.1 4.8 subtract_add_fusion
  186.9 1.9 copy-done.10
  188.9 3.6 convolution_convert_fusion.4
  192.8 5.9 convolution_convert_fusion.5
  198.7 6.4 reshape.203
  205.1 4.5 copy.48
  209.6 10.9 %fusion.5 = bf16[1024,2752]{0,1:T(8,128)(2,1)} fusion(bf16[1024,2752]{1,0:T(8,128)(2,1)} %get-tuple-element.22, bf16[1024,1024]{1,0:T(8,128)(2,1)} %bitcast.94), kind=kOutput, calls=%fused_computation.23 | convolution fusion | flops 5774180352 | bytes 13369344 | tf_op jit(solution)/shard_map/dot_general | solution.py:23
  220.7 0.8 copy-done.5
  221.5 28.2 %multiply_reduce_fusion = (f32[2,16,512]{2,1,0:T(8,128)S(1)}, f32[2,16,512,576]{2,3,1,0:T(8,128)}) fusion(f32[2,16,512,576]{2,3,1,0:T(8,128)} %get-tuple-element.30, f32[2,16,512]{2,1,0:T(8,128)S(1)} %copy-done.23, pred[2,512,576]{1,2,0:T(8,128)(4,1)S(1)} %copy-done.5, bf16[2,512,16,64]{1,3,2,0:T(8,128)(2,1)S(1)} %copy.48, bf16[2,576,16,64]{1,3,2,0:T(8,128)(2,1)} %bitcast.83), kind=kOutput, calls=%fused_computation.1 | convolution fusion | flops 1255129088 | bytes 80674816 | tf_op jit(solution)/shard_map/rqhe,rkhe->rhqk/dot_general | solution.py:102
  249.7 18.1 %fusion.23 = f32[2,16,64,576]{3,2,1,0:T(8,128)} fusion(bf16[2,512,16,64]{1,3,2,0:T(8,128)(2,1)S(1)} %copy.48, f32[2,16,512,576]{2,3,1,0:T(8,128)} %get-tuple-element.30, f32[2,16,512]{2,1,0:T(8,128)S(1)} %copy-done.23, pred[2,512,576]{1,2,0:T(8,128)(4,1)S(1)} %copy-done.5), kind=kOutput, calls=%fused_computation.65 | convolution fusion | flops 1245708288 | bytes 45219840 | tf_op jit(solution)/shard_map/rhqk,rqhe->rkhe/dot_general | solution.py:114
  267.7 5.8 copy.53
  273.6 32.1 %multiply_convert_fusion = bf16[2,16,512,576]{2,3,1,0:T(8,128)(2,1)} fusion(f32[2,16,512,576]{2,3,1,0:T(8,128)} %get-tuple-element.35, f32[2,16,512,576]{2,3,1,0:T(8,128)} %get-tuple-element.30, f32[2,16,512]{2,1,0:T(8,128)S(1)} %get-tuple-element.34, f32[2,16,512]{2,1,0:T(8,128)S(1)} %copy-done.23, pred[2,512,576]{1,2,0:T(8,128)(4,1)S(1)} %copy-done.5), kind=kLoop, calls=%fused_computation | loop fusion | flops 56623104 | bytes 95092736 | tf_op jit(solution)/shard_map/convert_element_type | solution.py:106
  305.7 12.1 %broadcast_multiply_fusion = f32[2,16,64,576]{3,2,1,0:T(8,128)} fusion(bf16[2,512,16,64]{1,3,2,0:T(8,128)(2,1)S(1)} %copy-done.3, bf16[2,16,512,576]{2,3,1,0:T(8,128)(2,1)} %multiply_convert_fusion), kind=kOutput, calls=%fused_computation.50 | convolution fusion | flops 1209139200 | bytes 25690112 | tf_op jit(solution)/shard_map/rhqk,rqhe->rkhe/dot_general | solution.py:111
  317.8 5.8 copy.52
  323.6 4.7 fusion.3
  328.3 0.9 slice.55
  329.2 1.7 collective-permute-start.1
  330.9 10.0 %fusion.17 = bf16[2,512,16,64]{1,3,2,0:T(8,128)(2,1)S(1)} fusion(bf16[2,576,16,64]{1,3,2,0:T(8,128)(2,1)S(1)} %bitcast.81, bf16[2,16,512,576]{2,3,1,0:T(8,128)(2,1)} %multiply_convert_fusion), kind=kOutput, calls=%fused_computation.57 | convolution fusion | flops 1210056704 | bytes 23330816 | tf_op jit(solution)/shard_map/rhqk,rkhe->rqhe/dot_general | solution.py:108
  340.9 4.7 copy.56
  345.7 5.5 reshape.199
  351.2 2.3 fusion.20
  353.4 1.0 slice-done
  354.4 0.6 pad_maximum_fusion.5
  355.0 2.0 copy-done.12
  357.1 9.1 %convolution_convert_fusion.2 = bf16[1024,3072]{1,0:T(8,128)(2,1)} fusion(bf16[1024,1024]{1,0:T(8,128)(2,1)S(1)} %copy-done.19, bf16[1024,2048]{1,0:T(8,128)(2,1)S(1)} %bitcast.88, bf16[1024,1024]{1,0:T(8,128)(2,1)S(1)} %reshape.199), kind=kOutput, calls=%fused_computation.21 | convolution fusion | flops 6458179584 | bytes 14680064 | tf_op jit(solution)/shard_map/dot_general | solution.py:23
  366.8 21.8 %convolution_convert_fusion = bf16[1024,5504]{1,0:T(8,128)(2,1)} fusion(bf16[1024,2752]{1,0:T(8,128)(2,1)} %get-tuple-element.21, bf16[1024,2752]{1,0:T(8,128)(2,1)} %get-tuple-element.20, f32[1024,1024]{1,0:T(8,128)} %copy-done.14, f32[1024]{0:T(1024)S(1)} %copy-done.32, f32[1024]{0:T(1024)S(1)} %copy-done.28), kind=kOutput, calls=%fused_computation.12 | convolution fusion | flops 11574050816 | bytes 26746880 | tf_op jit(solution)/shard_map/dot_general | solution.py:23
  388.7 0.6 copy-done.35
  389.3 0.6 dynamic-slice
  390.6 89.5 %reduce-scatter.5.cloned.1.call-done = bf16[256,3072]{1,0:T(8,128)(2,1)} async-done(((bf16[1024,3072]{1,0:T(8,128)(2,1)}), bf16[256,3072]{1,0:T(8,128)(2,1)}) %reduce-scatter.5.cloned.1.call-update) | async-done | bytes 1572880 | tf_op jit(solution)/shard_map/reduce_scatter | solution.py:138
  480.0 193.6 %reduce-scatter.9.cloned.1.call-done = bf16[256,5504]{1,0:T(8,128)(2,1)} async-done(((bf16[1024,5504]{1,0:T(8,128)(2,1)}), bf16[256,5504]{1,0:T(8,128)(2,1)}) %reduce-scatter.9.cloned.1.call-update) | async-done | bytes 2818064 | tf_op jit(solution)/shard_map/reduce_scatter | solution.py:144
  673.7 11.5 %add_convert_fusion = bf16[1024,1024]{1,0:T(8,128)(2,1)} fusion(f32[1024,1024]{1,0:T(8,128)} %copy-done.14, bf16[1024,2752]{1,0:T(8,128)(2,1)} %get-tuple-element.22, bf16[1024,2752]{0,1:T(8,128)(2,1)} %param.13), kind=kOutput, calls=%fused_computation.46 | convolution fusion | flops 5773459456 | bytes 17563648 | tf_op jit(solution)/shard_map/dot_general | solution.py:23
  685.3 12.0 %fusion.14 = (bf16[1024]{0:T(1024)(128)(2,1)S(1)}, f32[1024]{0:T(1024)S(1)}, f32[1024,1024]{1,0:T(8,128)}) fusion(bf16[2,512,1024]{2,1,0:T(8,128)(2,1)S(1)} %copy-done.8, f32[1024]{0:T(1024)S(1)} %bitcast.97, f32[1024]{0:T(1024)S(1)} %copy-done.29, bf16[1024,3072]{1,0:T(8,128)(2,1)} %param.10, bf16[1024,2048]{1,0:T(8,128)(2,1)S(1)} %bitcast.89, ...), kind=kOutput, calls=%fused_computation.41 | convolution fusion | flops 6462371840 | bytes 18888704 | tf_op jit(solution)/shard_map/dot_general | solution.py:23
  697.3 11.6 %all-reduce.4 = (bf16[1024]{0:T(1024)(128)(2,1)S(1)}, bf16[1024]{0:T(1024)(128)(2,1)S(1)}) all-reduce(bf16[1024]{0:T(1024)(128)(2,1)S(1)} %get-tuple-element.10, bf16[1024]{0:T(1024)(128)(2,1)S(1)} %copy-done.33), channel_id=6, replica_groups=mesh['dp'=8,'seq'=4] {'seq'}, use_global_device_ids=true, to_apply=%region_16.17.clone | all-reduce | flops 2048 | bytes 8192
  709.0 11.9 %all-reduce.2 = (bf16[256]{0:T(256)(128)(2,1)S(1)}, bf16[256]{0:T(256)(128)(2,1)S(1)}) all-reduce(bf16[256]{0:T(256)(128)(2,1)S(1)} %dynamic-slice.1, bf16[256]{0:T(256)(128)(2,1)S(1)} %dynamic-slice.3), channel_id=1, replica_groups=mesh['dp'=8,'seq'=4] {'dp'}, use_global_device_ids=true, to_apply=%region_17.18 | all-reduce | flops 512 | bytes 2048 | tf_op jit(solution)/shard_map/psum | solution.py:162
  722.0 5.4 fusion.11
  727.5 56.8 %all-reduce.7.cloned.1.call-done = (bf16[256,3072]{1,0:T(8,128)(2,1)}, bf16[256,1024]{1,0:T(8,128)(2,1)}, bf16[256,5504]{1,0:T(8,128)(2,1)}, bf16[256,2752]{0,1:T(8,128)(2,1)}) async-done(((bf16[256,3072]{1,0:T(8,128)(2,1)}, bf16[256,1024]{1,0:T(8,128)(2,1)}, bf16[256,5504]{1,0:T(8,128)(2,1)}, bf16[256,2752]{0,1:T(8,128)(2,1)}), (bf16[256,3072]{1,0:T(8,128)(2,1)}, bf16[256,1024]{1,0:T(8,128)(2,1)}, ...) | async-done | bytes 6324240 | tf_op jit(solution)/shard_map/psum | solution.py:158
  784.3 2.2 convert_element_type.125
  786.5 3.6 convert_element_type.123
  790.1 1.8 convert_element_type.130
  791.9 2.9 convert_element_type.127
  (95 shorter events, 4.2 us)
Async XLA Ops:
  7.2 109.8 %copy-start = (bf16[1024,1024]{1,0:T(8,128)(2,1)S(1)}, bf16[1024,1024]{1,0:T(8,128)(2,1)}, u32[]{:S(2)}) copy-start(bf16[1024,1024]{1,0:T(8,128)(2,1)} %param.11) | copy-start | bytes 6291460
  7.2 383.3 %reduce-scatter.7.cloned.1.call-start = ((), (), s32[]{:S(2)}) async-start(), calls=%async_computation.5 | async-start | bytes 2621440 | tf_op jit(solution)/shard_map/reduce_scatter | solution.py:141
  7.2 6.4 copy-start.34
  9.5 0.6 copy-start.25
  12.3 1.3 copy-start.18
  20.7 2.7 copy-start.11
  23.4 2.0 copy-start.6
  26.2 21.1 %collective-permute-start = (bf16[2,64,2048]{2,1,0:T(8,128)(2,1)}, bf16[2,64,2048]{2,1,0:T(8,128)(2,1)S(1)}, u32[]{:S(2)}, u32[]{:S(2)}) collective-permute-start(bf16[2,64,2048]{2,1,0:T(8,128)(2,1)} %slice.46), channel_id=1, source_target_pairs={{0,1},{1,2},{2,3},{4,5},{5,6},{6,7},{8,9},{9,10},{10,11},{12,13},{... | collective-permute-start | bytes 1572872 | tf_op jit(solution)/shard_map/ppermute | solution.py:19
  40.8 5.9 copy-start.30
  47.3 46.9 %copy-start.4 = (pred[2,512,576]{1,2,0:T(8,128)(4,1)}, pred[2,512,576]{1,2,0:T(8,128)(4,1)S(1)}, u32[]{:S(2)}) copy-start(pred[2,512,576]{1,2,0:T(8,128)(4,1)S(1)} %and_and_fusion) | copy-start | bytes 1769476
  94.2 18.2 %copy-start.22 = (f32[2,16,512]{2,1,0:T(8,128)}, f32[2,16,512]{2,1,0:T(8,128)S(1)}, u32[]{:S(2)}) copy-start(f32[2,16,512]{2,1,0:T(8,128)S(1)} %log_add_fusion) | copy-start | bytes 196612
  112.4 4.5 copy-start.7
  116.9 2.8 copy-start.20
  116.9 2.8 copy-start.31
  119.7 20.7 %copy-start.14 = (f32[1024,1024]{1,0:T(8,128)}, f32[1024,1024]{1,0:T(8,128)S(1)}, u32[]{:S(2)}) copy-start(f32[1024,1024]{1,0:T(8,128)S(1)} %get-tuple-element.32) | copy-start | bytes 12582916
  119.7 62.4 %copy-start.27 = (f32[1024]{0:T(1024)}, f32[1024]{0:T(1024)S(1)}, u32[]{:S(2)}) copy-start(f32[1024]{0:T(1024)S(1)} %get-tuple-element.28) | copy-start | bytes 12292
  182.1 6.7 copy-start.21
  186.9 1.9 copy-start.10
  192.5 198.0 %reduce-scatter.11.cloned.1.call-start = ((), (), s32[]{:S(2)}) async-start(), calls=%async_computation.7 | async-start | bytes 7045120 | tf_op jit(solution)/shard_map/reduce_scatter | solution.py:147
  220.4 1.1 copy-start.5
  220.4 1.1 copy-start.23
  220.5 259.6 %reduce-scatter.5.cloned.1.call-start = ((), (), s32[]{:S(2)}) async-start(), calls=%async_computation.4 | async-start | bytes 7864320 | tf_op jit(solution)/shard_map/reduce_scatter | solution.py:138
  273.6 32.1 %copy-start.3 = (bf16[2,512,16,64]{1,3,2,0:T(8,128)(2,1)S(1)}, bf16[2,512,16,64]{1,3,2,0:T(8,128)(2,1)}, u32[]{:S(2)}) copy-start(bf16[2,512,16,64]{1,3,2,0:T(8,128)(2,1)} %copy.43) | copy-start | bytes 6291460
  323.6 7.3 copy-start.2
  328.3 12.6 %copy-start.9 = (bf16[2,576,2048]{2,1,0:T(8,128)(2,1)}, bf16[2,576,2048]{2,1,0:T(8,128)(2,1)S(1)}, u32[]{:S(2)}) copy-start(bf16[2,576,2048]{2,1,0:T(8,128)(2,1)S(1)} %fusion.3) | copy-start | bytes 14155780
  329.2 21.9 %collective-permute-start.1 = (bf16[2,64,2048]{2,1,0:T(8,128)(2,1)}, bf16[2,64,2048]{2,1,0:T(8,128)(2,1)}, u32[]{:S(2)}, u32[]{:S(2)}) collective-permute-start(bf16[2,64,2048]{2,1,0:T(8,128)(2,1)} %slice.55), channel_id=1, source_target_pairs={{1,0},{2,1},{3,2},{5,4},{6,5},{7,6},{9,8},{10,9},{11,10},{13,12},{... | collective-permute-start | bytes 1572872 | tf_op jit(solution)/shard_map/ppermute | solution.py:19
  351.1 3.9 copy-start.16
  351.1 3.3 slice-start
  354.4 2.7 copy-start.19
  355.0 2.1 copy-start.12
  366.1 0.7 copy-start.28
  366.1 0.7 copy-start.32
  366.2 307.5 %reduce-scatter.9.cloned.1.call-start = ((), (), s32[]{:S(2)}) async-start(), calls=%async_computation.6 | async-start | bytes 14090240 | tf_op jit(solution)/shard_map/reduce_scatter | solution.py:144
  388.6 0.7 copy-start.35
  388.6 1.9 copy-start.26
  388.6 395.6 %all-reduce.7.cloned.1.call-start = ((), (), s32[]{:S(2)}) async-start(), calls=%async_computation.8 | async-start | bytes 12648448 | tf_op jit(solution)/shard_map/psum | solution.py:158
  673.7 11.6 %copy-start.8 = (bf16[2,512,1024]{2,1,0:T(8,128)(2,1)S(1)}, bf16[2,512,1024]{2,1,0:T(8,128)(2,1)}, u32[]{:S(2)}) copy-start(bf16[2,512,1024]{2,1,0:T(8,128)(2,1)} %param.9) | copy-start | bytes 6291460
  673.7 11.6 %copy-start.13 = (bf16[2,512,2048]{2,1,0:T(8,128)(2,1)S(1)}, bf16[2,512,2048]{2,1,0:T(8,128)(2,1)}, u32[]{:S(2)}) copy-start(bf16[2,512,2048]{2,1,0:T(8,128)(2,1)} %copy-done.12) | copy-start | bytes 12582916
  673.7 11.6 %copy-start.17 = (bf16[1024,1024]{1,0:T(8,128)(2,1)S(1)}, bf16[1024,1024]{1,0:T(8,128)(2,1)}, u32[]{:S(2)}) copy-start(bf16[1024,1024]{1,0:T(8,128)(2,1)} %copy-done.16) | copy-start | bytes 6291460
  673.7 11.6 %copy-start.29 = (f32[1024]{0:T(1024)S(1)}, f32[1024]{0:T(1024)}, u32[]{:S(2)}) copy-start(f32[1024]{0:T(1024)} %param.14) | copy-start | bytes 12292
  685.3 12.0 %copy-start.33 = (bf16[1024]{0:T(1024)(128)(2,1)S(1)}, bf16[1024]{0:T(1024)(128)(2,1)}, u32[]{:S(2)}) copy-start(bf16[1024]{0:T(1024)(128)(2,1)} %get-tuple-element.8) | copy-start | bytes 6148
  784.3 5.8 copy-start.24
  786.5 5.4 copy-start.15
  791.9 2.9 copy-start.1
Sparse Core Ops, SparseCore 0:
  192.7 44.0 reduce-scatter.6
  239.8 100.7 reduce-scatter.10
  366.3 113.6 reduce-scatter.4
  482.4 191.2 reduce-scatter.8
  677.6 106.5 all-reduce.6
where the time goes:
time: 806 us; the launch traced here: 801 us
  waiting for transfers between devices  340 us (42%)
  matrix products  251 us (31%)
  other arithmetic  87.6 us (11%)
  local copies, waits for them, and re-layouts  76.7 us (10%)
  blocking collectives  23.5 us (3%)
  between operations  15.2 us (2%)
    reduce_scatter x1, waiting for transfers between devices, per_device(): lax.psum_scatter(grad_gate_up.astype(jnp.bfloat16), 'seq', scatter_dimens...  194 us
    dot_general x8, matrix products, contract(): lax.dot_general(left, right, (((left_dim,), (right_dim,)), ((), ())), pre...  97.1 us
    reduce_scatter x1, waiting for transfers between devices, per_device(): lax.psum_scatter(grad_qkv.astype(jnp.bfloat16), 'seq', scatter_dimension=...  89.5 us
    psum x1, waiting for transfers between devices, per_device(): lax.psum(shares[0].astype(jnp.bfloat16), 'dp').astype(jnp.float32)  56.8 us
    convert_element_type x1, other arithmetic, per_device(): grad_scores = (prob_full * (grad_probs - weighted)).astype(jnp.bfloat16)  32.1 us
    dot_general x1, matrix products, per_device(): jnp.einsum('rqhe,rkhe->rhqk', grad_attended, values, preferred_element_ty...  28.2 us
    dot_general x1, matrix products, per_device(): gate_up = jnp.dot(normed_two, w_gate_up, preferred_element_type=jnp.float32)  20.6 us
    dot_general x1, matrix products, per_device(): grad_hidden = jnp.dot(grad_rows, w_down, preferred_element_type=jnp.float32)  19.4 us
  transfers between devices with their start and end apart: 7, of which 3 were waited for; matrix products, arithmetic and copies ran while one was open for 29% of the time, Pallas kernels for 0%

commit v1 on v0

--- a/solution.py
+++ b/solution.py
@@ -34,11 +34,101 @@
 
 def norm_back(grad_norm, values, inv_rms, gain):
     scaled = grad_norm * gain
-    gain_grad = jnp.sum(grad_norm * values * inv_rms, axis=0)
     input_grad = inv_rms * scaled - values * inv_rms**3 * jnp.mean(
         scaled * values, axis=-1, keepdims=True
     )
-    return (input_grad, gain_grad)
+    return input_grad
+
+
+def log2(count):
+    return count.bit_length() - 1
+
+
+def stage_orders(n_dp, n_seq):
+    dp = [("dp", bit) for bit in range(1, log2(n_dp))]
+    seq = [("seq", bit) for bit in range(log2(n_seq))]
+    return dp + seq, seq[:1] + dp[::-1] + seq[1:]
+
+
+def swap_pairs(n_dp, n_seq, steps):
+    pairs = []
+    for d in range(n_dp):
+        for s in range(n_seq):
+            axis, bit = steps[d % 2]
+            there = (d ^ (1 << bit), s) if axis == "dp" else (d, s ^ (1 << bit))
+            pairs.append((d * n_seq + s, there[0] * n_seq + there[1]))
+    return pairs
+
+
+def swap(value, steps):
+    n_dp, n_seq = lax.axis_size("dp"), lax.axis_size("seq")
+    return lax.ppermute(value, ("dp", "seq"), swap_pairs(n_dp, n_seq, steps))
+
+
+def bit_of(step):
+    axis, bit = step
+    return (lax.axis_index(axis) >> bit) & 1
+
+
+def own_bit(steps):
+    core = lax.axis_index("dp") & 1
+    return jnp.where(core == 0, bit_of(steps[0]), bit_of(steps[1]))
+
+
+CORE = (("dp", 0), ("dp", 0))
+
+
+def pick(value, index):
+    return lax.dynamic_index_in_dim(value, index, axis=0, keepdims=False)
+
+
+def scatter_sum(grad):
+    n_dp, n_seq = lax.axis_size("dp"), lax.axis_size("seq")
+    orders = stage_orders(n_dp, n_seq)
+    dims = [("seq", bit) for bit in reversed(range(log2(n_seq)))]
+    dims += [("dp", bit) for bit in reversed(range(1, log2(n_dp)))]
+    rows, columns = grad.shape
+    part = rows // (n_dp * n_seq)
+    cut = grad.reshape((2,) * len(dims) + (2, part, columns))
+    core = lax.axis_index("dp") & 1
+    halves = []
+    for which in range(2):
+        half = lax.index_in_dim(cut, which, axis=len(dims), keepdims=False)
+        order = [dims.index(step) for step in orders[which]]
+        halves.append(half.transpose(order + [len(dims), len(dims) + 1]))
+    first = jnp.where(core == 0, halves[1], halves[0])
+    kept = jnp.where(core == 0, halves[0], halves[1])
+    value = add(kept, swap(first, CORE))
+    for steps in zip(*orders):
+        bit = own_bit(steps)
+        got = swap(pick(value, 1 - bit), steps)
+        value = add(pick(value, bit), got)
+    return value
+
+
+def add(left, right):
+    return (left.astype(jnp.float32) + right.astype(jnp.float32)).astype(jnp.bfloat16)
+
+
+def gather_share(value):
+    n_dp, n_seq = lax.axis_size("dp"), lax.axis_size("seq")
+    orders = stage_orders(n_dp, n_seq)
+    dp_orders = [[step for step in order if step[0] == "dp"] for order in orders]
+    part, columns = value.shape
+    for steps in zip(*(order[::-1] for order in dp_orders)):
+        bit = own_bit(steps)
+        got = swap(value, steps)
+        value = jnp.stack([jnp.where(bit == 0, value, got), jnp.where(bit == 0, got, value)])
+    got = swap(value, CORE)
+    core = lax.axis_index("dp") & 1
+    halves = []
+    for which in range(2):
+        half = jnp.where(core == which, value, got)
+        dims = [("dp", bit) for bit in reversed(range(1, log2(n_dp)))]
+        order = [dp_orders[which].index(step) for step in dims]
+        halves.append(half.transpose(order + [len(dims), len(dims) + 1]))
+    whole = jnp.stack(halves, axis=len(dp_orders[0]))
+    return whole.reshape(n_dp * part, columns).astype(jnp.float32)
 
 
 def per_device(inputs, w_qkv, w_out, w_gate_up, w_down, gain_attn, gain_mlp, doc_start, cotangent):
@@ -86,8 +176,9 @@
     grad_gate = grad_hidden * up_act * sigma * (1.0 + gate_act * (1.0 - sigma))
     grad_up = grad_hidden * silu_gate
     grad_gu = jnp.concatenate([grad_gate, grad_up], axis=1).astype(jnp.bfloat16)
-    grad_gate_up = contract(normed_two, grad_gu, 0, 0)
-    grad_resid_in, grad_gain_mlp = norm_back(
+    grad_gate = contract(normed_two, grad_gu[:, :FF], 0, 0)
+    grad_up = contract(normed_two, grad_gu[:, FF:], 0, 0)
+    grad_resid_in = norm_back(
         contract(grad_gu, w_gate_up, 1, 1), resid, inv_two, gain_mlp
     )
     grad_resid = grad_rows.astype(jnp.float32) + grad_resid_in
@@ -130,39 +221,34 @@
         [grad_queries.reshape(tokens, width), own_grad.reshape(tokens, 2 * width)], axis=1
     ).astype(jnp.bfloat16)
     grad_qkv = contract(normed_one, grad_qkv_rows, 0, 0)
-    grad_flat, grad_gain_attn = norm_back(
+    grad_flat = norm_back(
         contract(grad_qkv_rows, w_qkv, 1, 1), flat, inv_one, gain_attn
     )
     grad_inputs = (grad_resid + grad_flat).reshape(rows, group, width)
-    shares = (
-        lax.psum_scatter(
-            grad_qkv.astype(jnp.bfloat16), "seq", scatter_dimension=0, tiled=True
-        ).astype(jnp.float32),
-        lax.psum_scatter(
-            grad_out.astype(jnp.bfloat16), "seq", scatter_dimension=0, tiled=True
-        ).astype(jnp.float32),
-        lax.psum_scatter(
-            grad_gate_up.astype(jnp.bfloat16), "seq", scatter_dimension=0, tiled=True
-        ).astype(jnp.float32),
-        lax.psum_scatter(
-            grad_down.astype(jnp.bfloat16), "seq", scatter_dimension=0, tiled=True
-        ).astype(jnp.float32),
-        lax.psum_scatter(
-            grad_gain_attn.astype(jnp.bfloat16), "seq", scatter_dimension=0, tiled=True
-        ).astype(jnp.float32),
-        lax.psum_scatter(
-            grad_gain_mlp.astype(jnp.bfloat16), "seq", scatter_dimension=0, tiled=True
-        ).astype(jnp.float32),
-    )
-    totals = (
-        lax.psum(shares[0].astype(jnp.bfloat16), "dp").astype(jnp.float32),
-        lax.psum(shares[1].astype(jnp.bfloat16), "dp").astype(jnp.float32),
-        lax.psum(shares[2].astype(jnp.bfloat16), "dp").astype(jnp.float32),
-        lax.psum(shares[3].astype(jnp.bfloat16), "dp").astype(jnp.float32),
-        lax.psum(shares[4].astype(jnp.bfloat16), "dp").astype(jnp.float32),
-        lax.psum(shares[5].astype(jnp.bfloat16), "dp").astype(jnp.float32),
-    )
-    return (outputs, grad_inputs, totals[0], totals[1], totals[2], totals[3], totals[4], totals[5])
+    shares = [
+        scatter_sum(grad.astype(jnp.bfloat16))
+        for grad in (grad_down, grad_gate, grad_up, jnp.concatenate([grad_out, grad_qkv], axis=1))
+    ]
+    total_down, total_gate, total_up, total_rest = [gather_share(share) for share in shares]
+    total_out, total_qkv = total_rest[:, :width], total_rest[:, width:]
+    total_gate_up = jnp.concatenate([total_gate, total_up], axis=1)
+    kept = total_qkv.shape[0]
+    first_row = lax.axis_index("seq") * kept
+
+    def gain_total(total, weight, gain):
+        mine = lax.dynamic_slice_in_dim(weight, first_row, kept, axis=0).astype(jnp.float32)
+        return jnp.sum(total * mine, axis=1) / lax.dynamic_slice_in_dim(gain, first_row, kept)
+
+    return (
+        outputs,
+        grad_inputs,
+        total_qkv,
+        total_out,
+        total_gate_up,
+        total_down,
+        gain_total(total_qkv, w_qkv, gain_attn),
+        gain_total(total_gate_up, w_gate_up, gain_mlp),
+    )
 
 
 def solution(mesh):

time: 806 us -> 669 us (0.83)
  waiting for transfers between devices: 340 us -> 128 us
  local copies, waits for them, and re-layouts: 76.7 us -> 141 us
  starting transfers between devices: 7.6 us -> 39.1 us
  other arithmetic: 87.6 us -> 117 us
  blocking collectives: 23.5 us -> 0 us
  matrix products: 251 us -> 231 us
  between operations: 15.2 us -> 2.31 us
    reduce_scatter x4 -> x0, waiting for transfers between devices: 283 us -> none  [the longest x1 194 us: per_device(): lax.psum_scatter(grad_gate_up.astype(jnp.bfloat16), 'seq', scatter_dimens...]
    ppermute x0 -> x32, waiting for transfers between devices: none -> 128 us  [swap(): return lax.ppermute(value, ('dp', 'seq'), swap_pairs(n_dp, n_seq, steps))]
    psum x1 -> x0, waiting for transfers between devices: 56.8 us -> none  [per_device(): lax.psum(shares[0].astype(jnp.bfloat16), 'dp').astype(jnp.float32)]
    ppermute x0 -> x32, starting transfers between devices: none -> 32.8 us  [swap(): return lax.ppermute(value, ('dp', 'seq'), swap_pairs(n_dp, n_seq, steps))]
    convert_element_type x0 -> x5, local copies, waits for them, and re-layouts: none -> 27.2 us  [the longest x3 24.9 us: per_device(): grad.astype(jnp.bfloat16)]
    dot_general x8 -> x9, matrix products: 97.1 us -> 81.5 us  [contract(): lax.dot_general(left, right, (((left_dim,), (right_dim,)), ((), ())), pre...]
    psum x1 -> x0, blocking collectives: 11.9 us -> none  [per_device(): lax.psum(shares[4].astype(jnp.bfloat16), 'dp').astype(jnp.float32)]
    unnamed x1 -> x0, blocking collectives: 11.6 us -> none
  transfers between devices with their start and end apart: 7 -> 34, of which waited for: 3 -> 14; matrix products, arithmetic and copies ran while one was open for 29% -> 20% of each run, Pallas kernels for 0% -> 0%
where the time goes in v1:
time: 669 us; the launch traced here: 658 us
  matrix products  231 us (35%)
  local copies, waits for them, and re-layouts  141 us (21%)
  waiting for transfers between devices  128 us (19%)
  other arithmetic  117 us (17%)
  starting transfers between devices  39.1 us (6%)
    ppermute x32, waiting for transfers between devices, swap(): return lax.ppermute(value, ('dp', 'seq'), swap_pairs(n_dp, n_seq, steps))  128 us
    dot_general x9, matrix products, contract(): lax.dot_general(left, right, (((left_dim,), (right_dim,)), ((), ())), pre...  81.5 us
    ppermute x32, starting transfers between devices, swap(): return lax.ppermute(value, ('dp', 'seq'), swap_pairs(n_dp, n_seq, steps))  32.8 us
    convert_element_type x1, other arithmetic, per_device(): grad_scores = (prob_full * (grad_probs - weighted)).astype(jnp.bfloat16)  31.5 us
    dot_general x1, matrix products, per_device(): jnp.einsum('rqhe,rkhe->rhqk', grad_attended, values, preferred_element_ty...  26.1 us
    convert_element_type x3, local copies, waits for them, and re-layouts, per_device(): grad.astype(jnp.bfloat16)  24.9 us
    unnamed x115, local copies, waits for them, and re-layouts  23.8 us
    convert_element_type x20, other arithmetic, add(): (left.astype(jnp.float32) + right.astype(jnp.float32)).astype(jnp.bfloat16)  20 us
  transfers between devices with their start and end apart: 34, of which 14 were waited for; matrix products, arithmetic and copies ran while one was open for 20% of the time, Pallas kernels for 0%

profile of v1, /device:TPU:0, one launch (start us, length us, event | category | flops | bytes accessed | tf_op | source)
XLA Modules:
  0.0 658.3 jit_solution(44702573170881792)
XLA Ops:
  7.0 7.1 %convolution_convert_fusion.3 = bf16[1024,3072]{1,0:T(8,128)(2,1)S(1)} fusion(bf16[1024,1024]{1,0:T(8,128)(2,1)S(1)} %fusion.20, bf16[1024,3072]{1,0:T(8,128)(2,1)S(1)} %copy-done.42), kind=kOutput, calls=%fused_computation.34 | convolution fusion | flops 6445596672 | bytes 14680064 | tf_op jit(solution)/shard_map/dot_general | solution.py:148
  19.6 4.9 collective-permute-start
  24.6 3.1 slice.97
  27.7 3.9 copy.152
  31.6 6.3 reshape.281
  38.0 5.5 copy.140
  44.5 4.2 pad_maximum_fusion.6
  48.7 4.3 copy.139
  53.1 4.3 copy.137
  57.4 17.4 %fusion = (f32[2,16,512]{2,1,0:T(8,128)S(1)}, f32[2,16,512,576]{2,3,1,0:T(8,128)}) fusion(pred[2,512,576]{1,2,0:T(8,128)(4,1)S(1)} %and_and_fusion, bf16[2,512,16,64]{1,3,2,0:T(8,128)(2,1)} %copy.140, bf16[2,576,16,64]{1,3,2,0:T(8,128)(2,1)} %bitcast.308), kind=kOutput, calls=%fused_computation.5 | convolution fusion | flops 1236254720 | bytes 42860544 | tf_op jit(solution)/shard_map/rqhe,rkhe->rhqk/dot_general | solution.py:30
  74.8 16.6 %exponential_reduce_fusion = f32[2,16,512]{2,1,0:T(8,128)S(1)} fusion(f32[2,16,512,576]{2,3,1,0:T(8,128)} %get-tuple-element.69, f32[2,16,512]{2,1,0:T(8,128)S(1)} %get-tuple-element.68, pred[2,512,576]{1,2,0:T(8,128)(4,1)S(1)} %and_and_fusion), kind=kLoop, calls=%fused_computation.3 | loop fusion | flops 37732352 | bytes 38469632 | tf_op jit(solution)/shard_map/reduce_sum | solution.py:157
  91.4 18.2 %convert_bitcast_fusion = bf16[2,512,16,64]{1,3,2,0:T(8,128)(2,1)} fusion(bf16[2,576,16,64]{1,3,2,0:T(8,128)(2,1)} %bitcast.312, f32[2,16,512,576]{2,3,1,0:T(8,128)} %get-tuple-element.69, f32[2,16,512]{2,1,0:T(8,128)S(1)} %log_add_fusion, pred[2,512,576]{1,2,0:T(8,128)(4,1)S(1)} %and_and_fusion), kind=kOutput, calls=%fused_computation.96 | convolution fusion | flops 1246756864 | bytes 42860544 | tf_op jit(solution)/shard_map/rhqk,rkhe->rqhe/dot_general | solution.py:159
  109.6 3.9 copy.141
  120.6 15.1 %fusion.70 = f32[1024,5504]{1,0:T(8,128)} fusion(bf16[1024,1024]{1,0:T(8,128)(2,1)S(1)} %multiply_convert_fusion.5, bf16[1024,5504]{1,0:T(8,128)(2,1)S(1)} %bitcast.333), kind=kOutput, calls=%fused_computation.204 | convolution fusion | flops 11542724608 | bytes 35913728 | tf_op jit(solution)/shard_map/dot_general | solution.py:164
  135.7 19.4 %multiply_convert_fusion.2 = (bf16[1024,2752]{1,0:T(8,128)(2,1)}, bf16[1024,2752]{1,0:T(8,128)(2,1)}, bf16[1024,2752]{1,0:T(8,128)(2,1)}) fusion(f32[1024,5504]{1,0:T(8,128)} %fusion.70, bf16[1024,1024]{1,0:T(8,128)(2,1)} %bitcast.330, bf16[1024,2752]{0,1:T(8,128)(2,1)} %param.13), kind=kOutput, calls=%fused_computation.8 | convolution fusion | flops 5813633024 | bytes 47185920 | tf_op jit(solution)/shard_map/dot_general | solution.py:175
  155.2 11.5 %add_convert_fusion.3 = bf16[1024,1024]{1,0:T(8,128)(2,1)} fusion(f32[1024,1024]{1,0:T(8,128)} %copy-done.16, bf16[1024,2752]{1,0:T(8,128)(2,1)} %get-tuple-element.38, bf16[1024,2752]{0,1:T(8,128)(2,1)} %param.13), kind=kOutput, calls=%fused_computation.61 | convolution fusion | flops 5773459456 | bytes 17563648 | tf_op jit(solution)/shard_map/dot_general | solution.py:23
  166.7 8.1 %fusion.14 = bf16[1024,2752]{0,1:T(8,128)(2,1)} fusion(bf16[1024,2752]{1,0:T(8,128)(2,1)S(1)} %copy-done.52, bf16[1024,1024]{1,0:T(8,128)(2,1)S(1)} %bitcast.331), kind=kOutput, calls=%fused_computation.36 | convolution fusion | flops 5774180352 | bytes 13369344 | tf_op jit(solution)/shard_map/dot_general | solution.py:23
  174.8 7.9 %convolution_convert_fusion.2 = bf16[1024,2752]{0,1:T(8,128)(2,1)} fusion(bf16[1024,1024]{1,0:T(8,128)(2,1)S(1)} %copy-done.37, bf16[1024,2752]{1,0:T(8,128)(2,1)S(1)} %copy-done.51), kind=kOutput, calls=%fused_computation.33 | convolution fusion | flops 5774180352 | bytes 13369344 | tf_op jit(solution)/shard_map/dot_general | solution.py:23
  182.8 20.6 %multiply_reduce_fusion.2 = (f32[1024]{0:T(1024)S(1)}, f32[1024,1024]{1,0:T(8,128)}) fusion(f32[1024,1024]{1,0:T(8,128)} %copy-done.16, f32[1024]{0:T(1024)S(1)} %copy-done.47, bf16[1024,5504]{1,0:T(8,128)(2,1)} %param.12, bf16[1024,2752]{1,0:T(8,128)(2,1)} %get-tuple-element.37, bf16[1024,2752]{1,0:T(8,128)(2,1)} %get-tuple-element.36), kind=kOutput, calls=%fused_computation.60 | convolution fusion | flops 11568413696 | bytes 30941184 | tf_op jit(solution)/shard_map/dot_general | solution.py:23
  203.4 10.9 %convolution_convert_fusion.1 = bf16[1024,2752]{0,1:T(8,128)(2,1)} fusion(bf16[1024,1024]{1,0:T(8,128)(2,1)} %copy-done.36, bf16[1024,2752]{1,0:T(8,128)(2,1)} %get-tuple-element.37), kind=kOutput, calls=%fused_computation.32 | convolution fusion | flops 5774180352 | bytes 13369344 | tf_op jit(solution)/shard_map/dot_general | solution.py:23
  217.8 3.7 convolution_convert_fusion.4
  221.5 6.5 reshape.282
  228.1 5.5 copy.145
  233.6 19.0 %fusion.58 = f32[2,16,64,576]{3,2,1,0:T(8,128)} fusion(bf16[2,512,16,64]{1,3,2,0:T(8,128)(2,1)} %copy.145, f32[2,16,512,576]{2,3,1,0:T(8,128)} %get-tuple-element.69, f32[2,16,512]{2,1,0:T(8,128)S(1)} %copy-done.41, pred[2,512,576]{1,2,0:T(8,128)(4,1)S(1)} %copy-done.11), kind=kOutput, calls=%fused_computation.183 | convolution fusion | flops 1245708288 | bytes 45219840 | tf_op jit(solution)/shard_map/rhqk,rqhe->rkhe/dot_general | solution.py:205
  252.6 26.1 %multiply_reduce_fusion = (f32[2,16,512]{2,1,0:T(8,128)S(1)}, f32[2,16,512,576]{2,3,1,0:T(8,128)}) fusion(f32[2,16,512,576]{2,3,1,0:T(8,128)} %get-tuple-element.69, f32[2,16,512]{2,1,0:T(8,128)S(1)} %copy-done.41, pred[2,512,576]{1,2,0:T(8,128)(4,1)S(1)} %copy-done.11, bf16[2,512,16,64]{1,3,2,0:T(8,128)(2,1)S(1)} %copy-done.21, ...), kind=kOutput, calls=%fused_computation.1 | convolution fusion | flops 1255129088 | bytes 80674816 | tf_op jit(solution)/shard_map/rqhe,rkhe->rhqk/dot_general | solution.py:193
  278.7 31.5 %multiply_convert_fusion = bf16[2,16,512,576]{2,3,1,0:T(8,128)(2,1)} fusion(f32[2,16,512,576]{2,3,1,0:T(8,128)} %get-tuple-element.75, f32[2,16,512,576]{2,3,1,0:T(8,128)} %get-tuple-element.69, f32[2,16,512]{2,1,0:T(8,128)S(1)} %get-tuple-element.74, f32[2,16,512]{2,1,0:T(8,128)S(1)} %copy-done.41, pred[2,512,576]{1,2,0:T(8,128)(4,1)S(1)} %copy-done.11), kind=kLoop, calls=%fused_computation | loop fusion | flops 56623104 | bytes 95092736 | tf_op jit(solution)/shard_map/convert_element_type | solution.py:197
  310.2 12.2 %fusion.37 = bf16[2,512,16,64]{1,3,2,0:T(8,128)(2,1)} fusion(bf16[2,576,16,64]{1,3,2,0:T(8,128)(2,1)} %bitcast.309, bf16[2,16,512,576]{2,3,1,0:T(8,128)(2,1)} %multiply_convert_fusion), kind=kOutput, calls=%fused_computation.99 | convolution fusion | flops 1210056704 | bytes 23330816 | tf_op jit(solution)/shard_map/rhqk,rkhe->rqhe/dot_general | solution.py:199
  322.4 12.4 %broadcast_multiply_fusion = f32[2,16,64,576]{3,2,1,0:T(8,128)} fusion(bf16[2,512,16,64]{1,3,2,0:T(8,128)(2,1)S(1)} %copy-done.3, bf16[2,16,512,576]{2,3,1,0:T(8,128)(2,1)} %multiply_convert_fusion), kind=kOutput, calls=%fused_computation.84 | convolution fusion | flops 1209139200 | bytes 25690112 | tf_op jit(solution)/shard_map/rhqk,rqhe->rkhe/dot_general | solution.py:202
  334.9 5.8 copy.150
  340.6 5.8 copy.149
  346.4 4.5 fusion.7
  353.2 8.3 %copy.175 = bf16[1024,2752]{1,0:T(8,128)(2,1)} copy(bf16[1024,2752]{0,1:T(8,128)(2,1)} %fusion.14) | data formatting | bytes 11272192 | tf_op jit(solution)/shard_map/convert_element_type | solution.py:229
  361.5 3.2 fusion.68
  373.0 8.3 %copy.168 = bf16[1024,2752]{1,0:T(8,128)(2,1)} copy(bf16[1024,2752]{0,1:T(8,128)(2,1)} %convolution_convert_fusion.1) | data formatting | bytes 11272192 | tf_op jit(solution)/shard_map/convert_element_type | solution.py:229
  381.3 5.7 fusion.69
  387.0 8.3 %copy.158 = bf16[1024,2752]{1,0:T(8,128)(2,1)} copy(bf16[1024,2752]{0,1:T(8,128)(2,1)} %convolution_convert_fusion.2) | data formatting | bytes 11272192 | tf_op jit(solution)/shard_map/convert_element_type | solution.py:229
  395.3 4.7 broadcast_select_fusion.1
  400.2 3.3 slice_bitcast_fusion.1
  406.9 6.3 copy.185
  413.2 6.5 reshape.280
  424.3 7.3 %fusion.11 = bf16[2,2,2,2,2,32,3072]{6,5,4,3,2,1,0:T(8,128)(2,1)S(1)} fusion(bf16[2,2,2,2,2,32,1024]{6,5,4,3,2,1,0:T(8,128)(2,1)S(1)} %bitcast.327, bf16[1024,2048]{1,0:T(8,128)(2,1)S(1)} %bitcast.324, bf16[1024,1024]{1,0:T(8,128)(2,1)S(1)} %copy-done.32), kind=kOutput, calls=%fused_computation.30 | convolution fusion | flops 6458179584 | bytes 14680064 | tf_op jit(solution)/shard_map/dot_general | solution.py:23
  431.6 9.0 %fusion.24 = (f32[1024]{0:T(1024)S(1)}, f32[1024,1024]{1,0:T(8,128)S(1)}) fusion(bf16[2,512,1024]{2,1,0:T(8,128)(2,1)S(1)} %copy-done.15, f32[1024]{0:T(1024)S(1)} %copy-done.48, bf16[1024,3072]{1,0:T(8,128)(2,1)} %param.10, bf16[1024,2048]{1,0:T(8,128)(2,1)S(1)} %bitcast.325, bf16[1024,1024]{1,0:T(8,128)(2,1)S(1)} %copy-done.32), kind=kOutput, calls=%fused_computation.57 | convolution fusion | flops 6459227136 | bytes 18882560 | tf_op jit(solution)/shard_map/dot_general | solution.py:23
  444.3 3.0 fusion.23
  448.5 3.3 add_convert_fusion.1
  454.6 4.9 add_convert_fusion.2
  463.2 3.2 fusion.10
  467.6 4.7 collective-permute-done.27
  474.3 13.5 %collective-permute-done.19 = bf16[2,2,2,32,2752]{4,3,2,1,0:T(8,128)(2,1)} collective-permute-done((bf16[2,2,2,32,2752]{4,3,2,1,0:T(8,128)(2,1)}, bf16[2,2,2,32,2752]{4,3,2,1,0:T(8,128)(2,1)}, u32[]{:S(2)}, u32[]{:S(2)}) %collective-permute-start.19) | collective-permute-done | bytes 1409056 | tf_op jit(solution)/shard_map/ppermute | solution.py:65
  491.2 12.0 %collective-permute-done.11 = bf16[2,2,2,32,2752]{4,3,0,1,2:T(8,128)(2,1)S(1)} collective-permute-done((bf16[2,2,2,32,2752]{4,3,0,1,2:T(8,128)(2,1)S(1)}, bf16[2,2,2,32,2752]{4,3,0,1,2:T(8,128)(2,1)S(1)}, u32[]{:S(2)}, u32[]{:S(2)}) %collective-permute-start.11) | collective-permute-done | bytes 1409056 | tf_op jit(solution)/shard_map/ppermute | solution.py:65
  505.3 3.9 add_convert_fusion
  514.1 9.2 %collective-permute-done.12 = bf16[2,2,32,2752]{3,2,0,1:T(8,128)(2,1)S(1)} collective-permute-done((bf16[2,2,32,2752]{3,2,0,1:T(8,128)(2,1)S(1)}, bf16[2,2,32,2752]{3,2,0,1:T(8,128)(2,1)S(1)}, u32[]{:S(2)}, u32[]{:S(2)}) %collective-permute-start.12) | collective-permute-done | bytes 704544 | tf_op jit(solution)/shard_map/ppermute | solution.py:65
  528.3 8.4 %collective-permute-done.21 = bf16[2,32,2752]{2,1,0:T(8,128)(2,1)S(1)} collective-permute-done((bf16[2,32,2752]{2,1,0:T(8,128)(2,1)S(1)}, bf16[2,32,2752]{2,1,0:T(8,128)(2,1)S(1)}, u32[]{:S(2)}, u32[]{:S(2)}) %collective-permute-start.21) | collective-permute-done | bytes 352288 | tf_op jit(solution)/shard_map/ppermute | solution.py:65
  539.0 9.3 %collective-permute-done.13 = bf16[2,32,2752]{2,1,0:T(8,128)(2,1)S(1)} collective-permute-done((bf16[2,32,2752]{2,1,0:T(8,128)(2,1)S(1)}, bf16[2,32,2752]{2,1,0:T(8,128)(2,1)S(1)}, u32[]{:S(2)}, u32[]{:S(2)}) %collective-permute-start.13) | collective-permute-done | bytes 352288 | tf_op jit(solution)/shard_map/ppermute | solution.py:65
  552.8 8.9 %collective-permute-done.14 = bf16[32,2752]{1,0:T(8,128)(2,1)S(1)} collective-permute-done((bf16[32,2752]{1,0:T(8,128)(2,1)S(1)}, bf16[32,2752]{1,0:T(8,128)(2,1)S(1)}, u32[]{:S(2)}, u32[]{:S(2)}) %collective-permute-start.14) | collective-permute-done | bytes 176160 | tf_op jit(solution)/shard_map/ppermute | solution.py:65
  564.7 4.7 collective-permute-done.15
  570.3 3.5 collective-permute-done.24
  574.0 3.6 collective-permute-done.16
  581.7 23.0 %collective-permute-done.4 = bf16[2,2,32,4096]{3,2,0,1:T(8,128)(2,1)S(1)} collective-permute-done((bf16[2,2,32,4096]{3,2,0,1:T(8,128)(2,1)S(1)}, bf16[2,2,32,4096]{3,2,0,1:T(8,128)(2,1)S(1)}, u32[]{:S(2)}, u32[]{:S(2)}) %collective-permute-start.4) | collective-permute-done | bytes 1048608 | tf_op jit(solution)/shard_map/ppermute | solution.py:65
  606.1 8.1 %collective-permute-done.5 = bf16[2,32,4096]{2,1,0:T(8,128)(2,1)S(1)} collective-permute-done((bf16[2,32,4096]{2,1,0:T(8,128)(2,1)S(1)}, bf16[2,32,4096]{2,1,0:T(8,128)(2,1)S(1)}, u32[]{:S(2)}, u32[]{:S(2)}) %collective-permute-start.5) | collective-permute-done | bytes 524320 | tf_op jit(solution)/shard_map/ppermute | solution.py:65
  615.4 11.3 %collective-permute-done.6 = bf16[32,4096]{1,0:T(8,128)(2,1)S(1)} collective-permute-done((bf16[32,4096]{1,0:T(8,128)(2,1)S(1)}, bf16[32,4096]{1,0:T(8,128)(2,1)S(1)}, u32[]{:S(2)}, u32[]{:S(2)}) %collective-permute-start.6) | collective-permute-done | bytes 262176 | tf_op jit(solution)/shard_map/ppermute | solution.py:65
  630.4 3.4 copy.181
  635.6 7.5 %collective-permute-done.8 = bf16[2,32,4096]{2,1,0:T(8,128)(2,1)S(1)} collective-permute-done((bf16[2,32,4096]{2,1,0:T(8,128)(2,1)S(1)}, bf16[2,32,4096]{2,1,0:T(8,128)(2,1)S(1)}, u32[]{:S(2)}, u32[]{:S(2)}) %collective-permute-start.8) | collective-permute-done | bytes 524320 | tf_op jit(solution)/shard_map/ppermute | solution.py:65
  644.7 5.7 multiply_reduce_fusion.1
  653.8 3.4 multiply_reduce_fusion.4
  (263 shorter events, 100.3 us)
Async XLA Ops:
  0.6 113.4 %copy-start = (bf16[1024,1024]{1,0:T(8,128)(2,1)S(1)}, bf16[1024,1024]{1,0:T(8,128)(2,1)}, u32[]{:S(2)}) copy-start(bf16[1024,1024]{1,0:T(8,128)(2,1)} %param.11) | copy-start | bytes 6291460
  0.6 6.4 copy-start.42
  19.6 24.9 %collective-permute-start = (bf16[2,64,2048]{2,1,0:T(8,128)(2,1)}, bf16[2,64,2048]{2,1,0:T(8,128)(2,1)S(1)}, u32[]{:S(2)}, u32[]{:S(2)}) collective-permute-start(bf16[2,64,2048]{2,1,0:T(8,128)(2,1)} %slice.94), channel_id=1, source_target_pairs={{0,1},{1,2},{2,3},{4,5},{5,6},{6,7},{8,9},{9,10},{10,11},{12,13},{... | collective-permute-start | bytes 1572872 | tf_op jit(solution)/shard_map/ppermute | solution.py:19
  38.0 5.9 copy-start.50
  44.5 46.9 %copy-start.10 = (pred[2,512,576]{1,2,0:T(8,128)(4,1)}, pred[2,512,576]{1,2,0:T(8,128)(4,1)S(1)}, u32[]{:S(2)}) copy-start(pred[2,512,576]{1,2,0:T(8,128)(4,1)S(1)} %and_and_fusion) | copy-start | bytes 1769476
  91.4 18.2 %copy-start.40 = (f32[2,16,512]{2,1,0:T(8,128)}, f32[2,16,512]{2,1,0:T(8,128)S(1)}, u32[]{:S(2)}) copy-start(f32[2,16,512]{2,1,0:T(8,128)S(1)} %log_add_fusion) | copy-start | bytes 196612
  114.0 5.4 slice-start
  114.1 6.5 slice-start.2
  120.6 15.1 %copy-start.36 = (bf16[1024,1024]{1,0:T(8,128)(2,1)}, bf16[1024,1024]{1,0:T(8,128)(2,1)S(1)}, u32[]{:S(2)}) copy-start(bf16[1024,1024]{1,0:T(8,128)(2,1)S(1)} %multiply_convert_fusion.5) | copy-start | bytes 6291460
  155.2 11.5 %copy-start.38 = (bf16[2,512,1024]{2,1,0:T(8,128)(2,1)S(1)}, bf16[2,512,1024]{2,1,0:T(8,128)(2,1)}, u32[]{:S(2)}) copy-start(bf16[2,512,1024]{2,1,0:T(8,128)(2,1)} %param.17) | copy-start | bytes 6291460
  155.2 11.5 %copy-start.52 = (bf16[1024,2752]{1,0:T(8,128)(2,1)S(1)}, bf16[1024,2752]{1,0:T(8,128)(2,1)}, u32[]{:S(2)}) copy-start(bf16[1024,2752]{1,0:T(8,128)(2,1)} %get-tuple-element.38) | copy-start | bytes 16908292
  166.7 8.1 %copy-start.37 = (bf16[1024,1024]{1,0:T(8,128)(2,1)S(1)}, bf16[1024,1024]{1,0:T(8,128)(2,1)}, u32[]{:S(2)}) copy-start(bf16[1024,1024]{1,0:T(8,128)(2,1)} %copy-done.36) | copy-start | bytes 6291460
  166.7 8.1 %copy-start.51 = (bf16[1024,2752]{1,0:T(8,128)(2,1)S(1)}, bf16[1024,2752]{1,0:T(8,128)(2,1)}, u32[]{:S(2)}) copy-start(bf16[1024,2752]{1,0:T(8,128)(2,1)} %get-tuple-element.36) | copy-start | bytes 16908292
  203.3 11.0 %copy-start.17 = (f32[1024,1024]{1,0:T(8,128)S(1)}, f32[1024,1024]{1,0:T(8,128)}, u32[]{:S(2)}) copy-start(f32[1024,1024]{1,0:T(8,128)} %copy-done.16) | copy-start | bytes 12582916
  203.3 11.0 %copy-start.28 = (f32[1024,1024]{1,0:T(8,128)S(1)}, f32[1024,1024]{1,0:T(8,128)}, u32[]{:S(2)}) copy-start(f32[1024,1024]{1,0:T(8,128)} %get-tuple-element.73) | copy-start | bytes 12582916
  203.3 11.0 %copy-start.39 = (bf16[2,512,1024]{2,1,0:T(8,128)(2,1)S(1)}, bf16[2,512,1024]{2,1,0:T(8,128)(2,1)}, u32[]{:S(2)}) copy-start(bf16[2,512,1024]{2,1,0:T(8,128)(2,1)} %param.17) | copy-start | bytes 6291460
  203.3 11.0 %copy-start.46 = (f32[1024]{0:T(1024)S(1)}, f32[1024]{0:T(1024)}, u32[]{:S(2)}) copy-start(f32[1024]{0:T(1024)} %copy-done.45) | copy-start | bytes 12292
  203.3 11.0 %copy-start.49 = (f32[1024]{0:T(1024)S(1)}, f32[1024]{0:T(1024)}, u32[]{:S(2)}) copy-start(f32[1024]{0:T(1024)} %get-tuple-element.66) | copy-start | bytes 12292
  228.1 5.5 copy-start.11
  228.1 5.5 copy-start.41
  233.6 19.0 %copy-start.12 = (bf16[2,576,1024]{1,2,0:T(8,128)(2,1)S(1)}, bf16[2,576,1024]{1,2,0:T(8,128)(2,1)}, u32[]{:S(2)}) copy-start(bf16[2,576,1024]{1,2,0:T(8,128)(2,1)} %copy.137) | copy-start | bytes 7077892
  233.6 19.0 %copy-start.21 = (bf16[2,512,16,64]{1,3,2,0:T(8,128)(2,1)S(1)}, bf16[2,512,16,64]{1,3,2,0:T(8,128)(2,1)}, u32[]{:S(2)}) copy-start(bf16[2,512,16,64]{1,3,2,0:T(8,128)(2,1)} %copy.145) | copy-start | bytes 6291460
  310.2 12.2 %copy-start.3 = (bf16[2,512,16,64]{1,3,2,0:T(8,128)(2,1)S(1)}, bf16[2,512,16,64]{1,3,2,0:T(8,128)(2,1)}, u32[]{:S(2)}) copy-start(bf16[2,512,16,64]{1,3,2,0:T(8,128)(2,1)} %copy.140) | copy-start | bytes 6291460
  364.7 5.9 copy-start.35
  369.0 78.3 %collective-permute-start.26 = (bf16[2,2,2,2,32,2752]{5,4,3,2,1,0:T(8,128)(2,1)}, bf16[2,2,2,2,32,2752]{5,4,3,2,1,0:T(8,128)(2,1)}, u32[]{:S(2)}, u32[]{:S(2)}) collective-permute-start(bf16[2,2,2,2,32,2752]{5,4,3,2,1,0:T(8,128)(2,1)} %broadcast_select_fusion.2), channel_id=1, source_target_pairs={{0,4},{1,5},{2,6},{3,7},{4,0},{5,1},{6,2},{7,3},{8,12},{9,13},{10,... | collective-permute-start | bytes 8454152 | tf_op jit(solution)/shard_map/ppermute | solution.py:65
  400.0 54.6 %collective-permute-start.18 = (bf16[2,2,2,2,32,2752]{5,4,3,2,1,0:T(8,128)(2,1)}, bf16[2,2,2,2,32,2752]{5,4,3,2,1,0:T(8,128)(2,1)}, u32[]{:S(2)}, u32[]{:S(2)}) collective-permute-start(bf16[2,2,2,2,32,2752]{5,4,3,2,1,0:T(8,128)(2,1)} %broadcast_select_fusion.1), channel_id=1, source_target_pairs={{0,4},{1,5},{2,6},{3,7},{4,0},{5,1},{6,2},{7,3},{8,12},{9,13},{10,... | collective-permute-start | bytes 8454152 | tf_op jit(solution)/shard_map/ppermute | solution.py:65
  403.5 16.2 %collective-permute-start.1 = (bf16[2,64,2048]{2,1,0:T(8,128)(2,1)S(1)}, bf16[2,64,2048]{2,1,0:T(8,128)(2,1)S(1)}, u32[]{:S(2)}, u32[]{:S(2)}) collective-permute-start(bf16[2,64,2048]{2,1,0:T(8,128)(2,1)S(1)} %slice.103), channel_id=1, source_target_pairs={{1,0},{2,1},{3,2},{5,4},{6,5},{7,6},{9,8},{10,9},{11,10},{13,12},{... | collective-permute-start | bytes 1572872 | tf_op jit(solution)/shard_map/ppermute | solution.py:19
  406.6 56.6 %collective-permute-start.10 = (bf16[2,2,2,2,32,2752]{5,4,0,1,2,3:T(8,128)(2,1)}, bf16[2,2,2,2,32,2752]{5,4,0,1,2,3:T(8,128)(2,1)}, u32[]{:S(2)}, u32[]{:S(2)}) collective-permute-start(bf16[2,2,2,2,32,2752]{5,4,0,1,2,3:T(8,128)(2,1)} %copy_select_fusion), channel_id=1, source_target_pairs={{0,4},{1,5},{2,6},{3,7},{4,0},{5,1},{6,2},{7,3},{8,12},{9,13},{10,... | collective-permute-start | bytes 8454152 | tf_op jit(solution)/shard_map/ppermute | solution.py:65
  424.3 7.3 %copy-start.15 = (bf16[2,512,1024]{2,1,0:T(8,128)(2,1)S(1)}, bf16[2,512,1024]{2,1,0:T(8,128)(2,1)}, u32[]{:S(2)}) copy-start(bf16[2,512,1024]{2,1,0:T(8,128)(2,1)} %param.9) | copy-start | bytes 6291460
  424.3 7.3 %copy-start.48 = (f32[1024]{0:T(1024)S(1)}, f32[1024]{0:T(1024)}, u32[]{:S(2)}) copy-start(f32[1024]{0:T(1024)} %param.14) | copy-start | bytes 12292
  444.0 61.2 %collective-permute-start.2 = (bf16[2,2,2,2,32,4096]{5,4,2,1,0,3:T(8,128)(2,1)}, bf16[2,2,2,2,32,4096]{5,4,2,1,0,3:T(8,128)(2,1)}, u32[]{:S(2)}, u32[]{:S(2)}) collective-permute-start(bf16[2,2,2,2,32,4096]{5,4,2,1,0,3:T(8,128)(2,1)} %broadcast_select_fusion), channel_id=1, source_target_pairs={{0,4},{1,5},{2,6},{3,7},{4,0},{5,1},{6,2},{7,3},{8,12},{9,13},{10,... | collective-permute-start | bytes 12582920 | tf_op jit(solution)/shard_map/ppermute | solution.py:65
  448.5 6.1 copy-start.9
  453.1 19.2 %collective-permute-start.27 = (bf16[2,2,2,32,2752]{4,3,2,1,0:T(8,128)(2,1)}, bf16[2,2,2,32,2752]{4,3,2,1,0:T(8,128)(2,1)S(1)}, u32[]{:S(2)}, u32[]{:S(2)}) collective-permute-start(bf16[2,2,2,32,2752]{4,3,2,1,0:T(8,128)(2,1)} %dynamic-slice_bitcast_fusion.1), channel_id=1, source_target_pairs={{0,8},{1,9},{2,10},{3,11},{4,5},{5,4},{6,7},{7,6},{8,0},{9,1},{10,... | collective-permute-start | bytes 4227080 | tf_op jit(solution)/shard_map/ppermute | solution.py:65
  454.6 8.6 %copy-start.24 = (bf16[2,2,2,2,32,2752]{5,4,0,1,2,3:T(8,128)(2,1)S(1)}, bf16[2,2,2,2,32,2752]{5,4,0,1,2,3:T(8,128)(2,1)}, u32[]{:S(2)}) copy-start(bf16[2,2,2,2,32,2752]{5,4,0,1,2,3:T(8,128)(2,1)} %get-tuple-element.43) | copy-start | bytes 8454148
  462.2 25.7 %collective-permute-start.19 = (bf16[2,2,2,32,2752]{4,3,2,1,0:T(8,128)(2,1)}, bf16[2,2,2,32,2752]{4,3,2,1,0:T(8,128)(2,1)}, u32[]{:S(2)}, u32[]{:S(2)}) collective-permute-start(bf16[2,2,2,32,2752]{4,3,2,1,0:T(8,128)(2,1)} %dynamic-slice_bitcast_fusion.2), channel_id=1, source_target_pairs={{0,8},{1,9},{2,10},{3,11},{4,5},{5,4},{6,7},{7,6},{8,0},{9,1},{10,... | collective-permute-start | bytes 4227080 | tf_op jit(solution)/shard_map/ppermute | solution.py:65
  466.4 21.5 %copy-start.25 = (bf16[2,2,2,2,32,2752]{5,4,3,2,1,0:T(8,128)(2,1)S(1)}, bf16[2,2,2,2,32,2752]{5,4,3,2,1,0:T(8,128)(2,1)}, u32[]{:S(2)}) copy-start(bf16[2,2,2,2,32,2752]{5,4,3,2,1,0:T(8,128)(2,1)} %add_convert_fusion.2) | copy-start | bytes 8454148
  466.5 36.7 %collective-permute-start.11 = (bf16[2,2,2,32,2752]{4,3,0,1,2:T(8,128)(2,1)S(1)}, bf16[2,2,2,32,2752]{4,3,0,1,2:T(8,128)(2,1)S(1)}, u32[]{:S(2)}, u32[]{:S(2)}) collective-permute-start(bf16[2,2,2,32,2752]{4,3,0,1,2:T(8,128)(2,1)S(1)} %dynamic-slice_bitcast_fusion.3), channel_id=1, source_target_pairs={{0,8},{1,9},{2,10},{3,11},{4,5},{5,4},{6,7},{7,6},{8,0},{9,1},{10,... | collective-permute-start | bytes 4227080 | tf_op jit(solution)/shard_map/ppermute | solution.py:65
  472.7 38.2 %collective-permute-start.28 = (bf16[2,2,32,2752]{3,2,1,0:T(8,128)(2,1)S(1)}, bf16[2,2,32,2752]{3,2,1,0:T(8,128)(2,1)S(1)}, u32[]{:S(2)}, u32[]{:S(2)}) collective-permute-start(bf16[2,2,32,2752]{3,2,1,0:T(8,128)(2,1)S(1)} %dynamic-slice_bitcast_fusion.5), channel_id=1, source_target_pairs={{0,16},{1,17},{2,18},{3,19},{4,20},{5,21},{6,22},{7,23},{8,24},{9,... | collective-permute-start | bytes 2113544 | tf_op jit(solution)/shard_map/ppermute | solution.py:65
  489.7 24.2 %collective-permute-start.20 = (bf16[2,2,32,2752]{3,2,1,0:T(8,128)(2,1)S(1)}, bf16[2,2,32,2752]{3,2,1,0:T(8,128)(2,1)S(1)}, u32[]{:S(2)}, u32[]{:S(2)}) collective-permute-start(bf16[2,2,32,2752]{3,2,1,0:T(8,128)(2,1)S(1)} %dynamic-slice_bitcast_fusion.6), channel_id=1, source_target_pairs={{0,16},{1,17},{2,18},{3,19},{4,20},{5,21},{6,22},{7,23},{8,24},{9,... | collective-permute-start | bytes 2113544 | tf_op jit(solution)/shard_map/ppermute | solution.py:65
  503.7 19.7 %collective-permute-start.12 = (bf16[2,2,32,2752]{3,2,0,1:T(8,128)(2,1)S(1)}, bf16[2,2,32,2752]{3,2,0,1:T(8,128)(2,1)S(1)}, u32[]{:S(2)}, u32[]{:S(2)}) collective-permute-start(bf16[2,2,32,2752]{3,2,0,1:T(8,128)(2,1)S(1)} %dynamic-slice_bitcast_fusion.7), channel_id=1, source_target_pairs={{0,16},{1,17},{2,18},{3,19},{4,20},{5,21},{6,22},{7,23},{8,24},{9,... | collective-permute-start | bytes 2113544 | tf_op jit(solution)/shard_map/ppermute | solution.py:65
  509.3 68.8 %collective-permute-start.3 = (bf16[2,2,2,32,4096]{4,3,1,0,2:T(8,128)(2,1)S(1)}, bf16[2,2,2,32,4096]{4,3,1,0,2:T(8,128)(2,1)S(1)}, u32[]{:S(2)}, u32[]{:S(2)}) collective-permute-start(bf16[2,2,2,32,4096]{4,3,1,0,2:T(8,128)(2,1)S(1)} %dynamic-slice_bitcast_fusion), channel_id=1, source_target_pairs={{0,8},{1,9},{2,10},{3,11},{4,5},{5,4},{6,7},{7,6},{8,0},{9,1},{10,... | collective-permute-start | bytes 6291464 | tf_op jit(solution)/shard_map/ppermute | solution.py:65
  511.1 14.4 %collective-permute-start.29 = (bf16[2,32,2752]{2,1,0:T(8,128)(2,1)S(1)}, bf16[2,32,2752]{2,1,0:T(8,128)(2,1)S(1)}, u32[]{:S(2)}, u32[]{:S(2)}) collective-permute-start(bf16[2,32,2752]{2,1,0:T(8,128)(2,1)S(1)} %dynamic-slice_bitcast_fusion.9), channel_id=1, source_target_pairs={{0,1},{1,0},{2,3},{3,2},{4,12},{5,13},{6,14},{7,15},{8,9},{9,8},{1... | collective-permute-start | bytes 1056776 | tf_op jit(solution)/shard_map/ppermute | solution.py:65
  514.0 22.6 %collective-permute-start.21 = (bf16[2,32,2752]{2,1,0:T(8,128)(2,1)S(1)}, bf16[2,32,2752]{2,1,0:T(8,128)(2,1)S(1)}, u32[]{:S(2)}, u32[]{:S(2)}) collective-permute-start(bf16[2,32,2752]{2,1,0:T(8,128)(2,1)S(1)} %dynamic-slice_bitcast_fusion.10), channel_id=1, source_target_pairs={{0,1},{1,0},{2,3},{3,2},{4,12},{5,13},{6,14},{7,15},{8,9},{9,8},{1... | collective-permute-start | bytes 1056776 | tf_op jit(solution)/shard_map/ppermute | solution.py:65
  523.6 24.7 %collective-permute-start.13 = (bf16[2,32,2752]{2,1,0:T(8,128)(2,1)S(1)}, bf16[2,32,2752]{2,1,0:T(8,128)(2,1)S(1)}, u32[]{:S(2)}, u32[]{:S(2)}) collective-permute-start(bf16[2,32,2752]{2,1,0:T(8,128)(2,1)S(1)} %dynamic-slice_bitcast_fusion.11), channel_id=1, source_target_pairs={{0,1},{1,0},{2,3},{3,2},{4,12},{5,13},{6,14},{7,15},{8,9},{9,8},{1... | collective-permute-start | bytes 1056776 | tf_op jit(solution)/shard_map/ppermute | solution.py:65
  525.6 25.0 %collective-permute-start.30 = (bf16[32,2752]{1,0:T(8,128)(2,1)S(1)}, bf16[32,2752]{1,0:T(8,128)(2,1)S(1)}, u32[]{:S(2)}, u32[]{:S(2)}) collective-permute-start(bf16[32,2752]{1,0:T(8,128)(2,1)S(1)} %dynamic-slice_bitcast_fusion.13), channel_id=1, source_target_pairs={{0,2},{1,3},{2,0},{3,1},{4,6},{5,7},{6,4},{7,5},{8,10},{9,11},{10,... | collective-permute-start | bytes 528392 | tf_op jit(solution)/shard_map/ppermute | solution.py:65
  536.8 14.4 %collective-permute-start.22 = (bf16[32,2752]{1,0:T(8,128)(2,1)S(1)}, bf16[32,2752]{1,0:T(8,128)(2,1)S(1)}, u32[]{:S(2)}, u32[]{:S(2)}) collective-permute-start(bf16[32,2752]{1,0:T(8,128)(2,1)S(1)} %dynamic-slice_bitcast_fusion.14), channel_id=1, source_target_pairs={{0,2},{1,3},{2,0},{3,1},{4,6},{5,7},{6,4},{7,5},{8,10},{9,11},{10,... | collective-permute-start | bytes 528392 | tf_op jit(solution)/shard_map/ppermute | solution.py:65
  548.4 13.3 %collective-permute-start.14 = (bf16[32,2752]{1,0:T(8,128)(2,1)S(1)}, bf16[32,2752]{1,0:T(8,128)(2,1)S(1)}, u32[]{:S(2)}, u32[]{:S(2)}) collective-permute-start(bf16[32,2752]{1,0:T(8,128)(2,1)S(1)} %dynamic-slice_bitcast_fusion.15), channel_id=1, source_target_pairs={{0,2},{1,3},{2,0},{3,1},{4,6},{5,7},{6,4},{7,5},{8,10},{9,11},{10,... | collective-permute-start | bytes 528392 | tf_op jit(solution)/shard_map/ppermute | solution.py:65
  550.6 11.7 %collective-permute-start.31 = (bf16[32,2752]{1,0:T(8,128)(2,1)S(1)}, bf16[32,2752]{1,0:T(8,128)(2,1)S(1)}, u32[]{:S(2)}, u32[]{:S(2)}) collective-permute-start(bf16[32,2752]{1,0:T(8,128)(2,1)S(1)} %fusion.55), channel_id=1, source_target_pairs={{0,16},{1,17},{2,18},{3,19},{4,12},{5,13},{6,14},{7,15},{8,24},{9,... | collective-permute-start | bytes 528392 | tf_op jit(solution)/shard_map/ppermute | solution.py:65
  551.3 11.8 %collective-permute-start.23 = (bf16[32,2752]{1,0:T(8,128)(2,1)S(1)}, bf16[32,2752]{1,0:T(8,128)(2,1)S(1)}, u32[]{:S(2)}, u32[]{:S(2)}) collective-permute-start(bf16[32,2752]{1,0:T(8,128)(2,1)S(1)} %fusion.56), channel_id=1, source_target_pairs={{0,16},{1,17},{2,18},{3,19},{4,12},{5,13},{6,14},{7,15},{8,24},{9,... | collective-permute-start | bytes 528392 | tf_op jit(solution)/shard_map/ppermute | solution.py:65
  561.8 7.6 %collective-permute-start.15 = (bf16[32,2752]{1,0:T(8,128)(2,1)S(1)}, bf16[32,2752]{1,0:T(8,128)(2,1)S(1)}, u32[]{:S(2)}, u32[]{:S(2)}) collective-permute-start(bf16[32,2752]{1,0:T(8,128)(2,1)S(1)} %fusion.57), channel_id=1, source_target_pairs={{0,16},{1,17},{2,18},{3,19},{4,12},{5,13},{6,14},{7,15},{8,24},{9,... | collective-permute-start | bytes 528392 | tf_op jit(solution)/shard_map/ppermute | solution.py:65
  562.4 7.6 %collective-permute-start.32 = (bf16[2,32,2752]{2,1,0:T(8,128)(2,1)S(1)}, bf16[2,32,2752]{2,1,0:T(8,128)(2,1)S(1)}, u32[]{:S(2)}, u32[]{:S(2)}) collective-permute-start(bf16[2,32,2752]{2,1,0:T(8,128)(2,1)S(1)} %pad_maximum_fusion.16), channel_id=1, source_target_pairs={{0,8},{1,9},{2,10},{3,11},{4,20},{5,21},{6,22},{7,23},{8,0},{9,1},... | collective-permute-start | bytes 1056776 | tf_op jit(solution)/shard_map/ppermute | solution.py:65
  563.1 10.6 %collective-permute-start.24 = (bf16[2,32,2752]{2,1,0:T(8,128)(2,1)S(1)}, bf16[2,32,2752]{2,1,0:T(8,128)(2,1)S(1)}, u32[]{:S(2)}, u32[]{:S(2)}) collective-permute-start(bf16[2,32,2752]{2,1,0:T(8,128)(2,1)S(1)} %pad_maximum_fusion.15), channel_id=1, source_target_pairs={{0,8},{1,9},{2,10},{3,11},{4,20},{5,21},{6,22},{7,23},{8,0},{9,1},... | collective-permute-start | bytes 1056776 | tf_op jit(solution)/shard_map/ppermute | solution.py:65
  569.4 8.2 %collective-permute-start.16 = (bf16[2,32,2752]{2,1,0:T(8,128)(2,1)S(1)}, bf16[2,32,2752]{2,1,0:T(8,128)(2,1)S(1)}, u32[]{:S(2)}, u32[]{:S(2)}) collective-permute-start(bf16[2,32,2752]{2,1,0:T(8,128)(2,1)S(1)} %pad_maximum_fusion.14), channel_id=1, source_target_pairs={{0,8},{1,9},{2,10},{3,11},{4,20},{5,21},{6,22},{7,23},{8,0},{9,1},... | collective-permute-start | bytes 1056776 | tf_op jit(solution)/shard_map/ppermute | solution.py:65
  570.2 7.7 %collective-permute-start.33 = (bf16[2,2,32,2752]{3,2,1,0:T(8,128)(2,1)S(1)}, bf16[2,2,32,2752]{3,2,1,0:T(8,128)(2,1)S(1)}, u32[]{:S(2)}, u32[]{:S(2)}) collective-permute-start(bf16[2,2,32,2752]{3,2,1,0:T(8,128)(2,1)S(1)} %pad_maximum_fusion.12), channel_id=1, source_target_pairs={{0,4},{1,5},{2,6},{3,7},{4,0},{5,1},{6,2},{7,3},{8,12},{9,13},{10,... | collective-permute-start | bytes 2113544 | tf_op jit(solution)/shard_map/ppermute | solution.py:65
  574.0 6.7 %collective-permute-start.25 = (bf16[2,2,32,2752]{3,2,0,1:T(8,128)(2,1)S(1)}, bf16[2,2,32,2752]{3,2,0,1:T(8,128)(2,1)S(1)}, u32[]{:S(2)}, u32[]{:S(2)}) collective-permute-start(bf16[2,2,32,2752]{3,2,0,1:T(8,128)(2,1)S(1)} %copy.172), channel_id=1, source_target_pairs={{0,4},{1,5},{2,6},{3,7},{4,0},{5,1},{6,2},{7,3},{8,12},{9,13},{10,... | collective-permute-start | bytes 2113544 | tf_op jit(solution)/shard_map/ppermute | solution.py:65
  577.8 36.6 %collective-permute-start.17 = (bf16[2,2,32,2752]{3,2,0,1:T(8,128)(2,1)S(1)}, bf16[2,2,32,2752]{3,2,0,1:T(8,128)(2,1)S(1)}, u32[]{:S(2)}, u32[]{:S(2)}) collective-permute-start(bf16[2,2,32,2752]{3,2,0,1:T(8,128)(2,1)S(1)} %copy.165), channel_id=1, source_target_pairs={{0,4},{1,5},{2,6},{3,7},{4,0},{5,1},{6,2},{7,3},{8,12},{9,13},{10,... | collective-permute-start | bytes 2113544 | tf_op jit(solution)/shard_map/ppermute | solution.py:65
  579.0 25.6 %collective-permute-start.4 = (bf16[2,2,32,4096]{3,2,0,1:T(8,128)(2,1)S(1)}, bf16[2,2,32,4096]{3,2,0,1:T(8,128)(2,1)S(1)}, u32[]{:S(2)}, u32[]{:S(2)}) collective-permute-start(bf16[2,2,32,4096]{3,2,0,1:T(8,128)(2,1)S(1)} %dynamic-slice_bitcast_fusion.4), channel_id=1, source_target_pairs={{0,16},{1,17},{2,18},{3,19},{4,20},{5,21},{6,22},{7,23},{8,24},{9,... | collective-permute-start | bytes 3145736 | tf_op jit(solution)/shard_map/ppermute | solution.py:65
  605.0 9.2 %collective-permute-start.5 = (bf16[2,32,4096]{2,1,0:T(8,128)(2,1)S(1)}, bf16[2,32,4096]{2,1,0:T(8,128)(2,1)S(1)}, u32[]{:S(2)}, u32[]{:S(2)}) collective-permute-start(bf16[2,32,4096]{2,1,0:T(8,128)(2,1)S(1)} %dynamic-slice_bitcast_fusion.8), channel_id=1, source_target_pairs={{0,1},{1,0},{2,3},{3,2},{4,12},{5,13},{6,14},{7,15},{8,9},{9,8},{1... | collective-permute-start | bytes 1572872 | tf_op jit(solution)/shard_map/ppermute | solution.py:65
  614.4 12.4 %collective-permute-start.6 = (bf16[32,4096]{1,0:T(8,128)(2,1)S(1)}, bf16[32,4096]{1,0:T(8,128)(2,1)S(1)}, u32[]{:S(2)}, u32[]{:S(2)}) collective-permute-start(bf16[32,4096]{1,0:T(8,128)(2,1)S(1)} %dynamic-slice_bitcast_fusion.12), channel_id=1, source_target_pairs={{0,2},{1,3},{2,0},{3,1},{4,6},{5,7},{6,4},{7,5},{8,10},{9,11},{10,... | collective-permute-start | bytes 786440 | tf_op jit(solution)/shard_map/ppermute | solution.py:65
  626.8 6.9 %collective-permute-start.7 = (bf16[32,4096]{1,0:T(8,128)(2,1)S(1)}, bf16[32,4096]{1,0:T(8,128)(2,1)S(1)}, u32[]{:S(2)}, u32[]{:S(2)}) collective-permute-start(bf16[32,4096]{1,0:T(8,128)(2,1)S(1)} %fusion.54), channel_id=1, source_target_pairs={{0,16},{1,17},{2,18},{3,19},{4,12},{5,13},{6,14},{7,15},{8,24},{9,... | collective-permute-start | bytes 786440 | tf_op jit(solution)/shard_map/ppermute | solution.py:65
  633.9 9.6 %copy-start.29 = (bf16[2,2,1,32,2752]{4,3,1,0,2:T(8,128)(2,1)S(1)}, bf16[2,2,1,32,2752]{4,3,1,0,2:T(8,128)(2,1)}, u32[]{:S(2)}) copy-start(bf16[2,2,1,32,2752]{4,3,1,0,2:T(8,128)(2,1)} %fusion.52) | copy-start | bytes 2113540
  633.9 9.6 %copy-start.30 = (bf16[2,2,1,32,2752]{4,3,1,0,2:T(8,128)(2,1)S(1)}, bf16[2,2,1,32,2752]{4,3,1,0,2:T(8,128)(2,1)}, u32[]{:S(2)}) copy-start(bf16[2,2,1,32,2752]{4,3,1,0,2:T(8,128)(2,1)} %select_bitcast_fusion.2) | copy-start | bytes 2113540
  633.9 9.2 %collective-permute-start.8 = (bf16[2,32,4096]{2,1,0:T(8,128)(2,1)S(1)}, bf16[2,32,4096]{2,1,0:T(8,128)(2,1)S(1)}, u32[]{:S(2)}, u32[]{:S(2)}) collective-permute-start(bf16[2,32,4096]{2,1,0:T(8,128)(2,1)S(1)} %pad_maximum_fusion.13), channel_id=1, source_target_pairs={{0,8},{1,9},{2,10},{3,11},{4,20},{5,21},{6,22},{7,23},{8,0},{9,1},... | collective-permute-start | bytes 1572872 | tf_op jit(solution)/shard_map/ppermute | solution.py:65
  643.4 8.2 %collective-permute-start.9 = (bf16[2,2,32,4096]{3,2,0,1:T(8,128)(2,1)S(1)}, bf16[2,2,32,4096]{3,2,0,1:T(8,128)(2,1)S(1)}, u32[]{:S(2)}, u32[]{:S(2)}) collective-permute-start(bf16[2,2,32,4096]{3,2,0,1:T(8,128)(2,1)S(1)} %copy.155), channel_id=1, source_target_pairs={{0,4},{1,5},{2,6},{3,7},{4,0},{5,1},{6,2},{7,3},{8,12},{9,13},{10,... | collective-permute-start | bytes 3145736 | tf_op jit(solution)/shard_map/ppermute | solution.py:65
  (26 other events, 79.8 us)
